TPU v7x, 32 devices: a whole 2x2x4 slice. The times are simulated.
32 devices in a mesh: dp: 2 (over x), expert: 8 (over z, core), tensor: 2 (over y).
Axes of the slice: x: 2, y: 2, z: 4, core: 2. Of those that a mesh axis runs over, the one named last changes fastest.
Arguments:
- tokens: bfloat16 [256, 2048], P(('dp', 'expert')), may hold values from -6 to 6
- routes: int32 [256, 8], P(('dp', 'expert')), may hold values from 0 to 15, all different within a row; in each aligned block of 16 rows (0 to 15, 16 to 31, ...) at most 16 rows name the same one
- route_weight: float32 [256, 8], P(('dp', 'expert')), may hold values from 0.02 to 0.5
- weights_gate_up: bfloat16 [16, 2048, 2, 768], P('expert', None, None, 'tensor'), may hold values from -0.125 to 0.125
- weights_down: bfloat16 [16, 2048, 768], P('expert', None, 'tensor'), may hold values from -0.21875 to 0.21875
- cotangent: bfloat16 [256, 2048], P(('dp', 'expert')), may hold values from -6 to 6
Outputs:
- layer_out: bfloat16 [256, 2048], P(('dp', 'expert'), 'tensor')
- tokens_grad: bfloat16 [256, 2048], P(('dp', 'expert'), 'tensor')
- gate_up_grad: bfloat16 [16, 2048, 2, 768], P('expert', 'dp', None, 'tensor')
- down_grad: bfloat16 [16, 2048, 768], P('expert', 'dp', 'tensor')
Inputs may be any that keep to these rules, and one draw needn't show every extreme that they name: `routes`: each row names 8 different experts. Among the 16 rows of one index of dp and expert no expert is named more than 16 times, a bound that some block reaches.
All inputs are finite; a program needn't handle non-finite values.
Results may differ from a plain program's by a relative error of at most 0.0072.
Values may be sent and summed in bfloat16 or wider, within the bound.
A program may use at most 64 MiB of HBM per device.

v0:
```python
import jax
import jax.numpy as jnp
from jax import lax
from jax.sharding import PartitionSpec as P

F32 = jnp.float32
BF16 = jnp.bfloat16


def cut(value):
    return lax.reduce_precision(value, exponent_bits=8, mantissa_bits=7)


def body(tokens, routes, route_weight, weights_gate_up, weights_down, cotangent):
    tok_rows, width = tokens.shape
    expert_local = weights_gate_up.shape[0]
    n_expert = lax.axis_size("expert")
    n_tensor = lax.axis_size("tensor")
    n_dp = lax.axis_size("dp")
    expert_total = expert_local * n_expert
    group = tok_rows * n_expert
    my_dp = lax.axis_index("dp")
    chosen = routes[:, :, None] == jnp.arange(expert_total, dtype=jnp.int32)[None, None, :]
    dense = jnp.sum(jnp.where(chosen, route_weight[:, :, None], 0.0), axis=1)
    first = cut(dense)
    second = cut(dense - first)
    third = dense - first - second
    parts = jnp.concatenate([first, second, third], axis=1).astype(BF16)
    spare = -parts.shape[1] % 128
    parts = jnp.pad(parts, ((0, 0), (0, spare)))
    sent = jnp.concatenate([tokens, cotangent, parts], axis=1)
    held = lax.all_gather(sent, "expert", axis=0, tiled=True)
    tok = held[:, :width]
    cot = held[:, width : 2 * width]
    parts = held[:, 2 * width : 2 * width + 3 * expert_total].astype(F32)
    parts = parts.reshape(group, 3, expert_total)
    weight = parts[:, 0] + parts[:, 1] + parts[:, 2]
    weight = lax.dynamic_slice_in_dim(
        weight, lax.axis_index("expert") * expert_local, expert_local, axis=1
    ).T[:, :, None]
    share = width // n_dp

    def columns(shift):
        start = lax.rem(my_dp + shift, n_dp) * share
        return jnp.concatenate(
            [
                lax.dynamic_slice_in_dim(tok, start, share, axis=1),
                lax.dynamic_slice_in_dim(cot, start, share, axis=1),
            ],
            axis=1,
        )

    def moved(value, shift):
        return lax.ppermute(value, "dp", [(i, (i + shift) % n_dp) for i in range(n_dp)])

    sides = [columns(0)] + [moved(columns(s), s) for s in range(1, n_dp)]
    gate_up = jnp.einsum("td,edgh->etgh", tok, weights_gate_up, preferred_element_type=F32)
    gate_pre = gate_up[:, :, 0, :]
    up_pre = gate_up[:, :, 1, :]
    sig_gate = jax.nn.sigmoid(gate_pre)
    silu_gate = gate_pre * sig_gate
    hidden = (silu_gate * up_pre * weight).astype(BF16)
    hidden_grad = weight * jnp.einsum("td,edh->eth", cot, weights_down, preferred_element_type=F32)
    gate_grad = (hidden_grad * up_pre * sig_gate * (1.0 + gate_pre * (1.0 - sig_gate))).astype(BF16)
    up_grad = (hidden_grad * silu_gate).astype(BF16)
    mine = jnp.stack([gate_grad, up_grad, hidden], axis=0)
    acts = jnp.concatenate([mine] + [moved(mine, s) for s in range(1, n_dp)], axis=2)
    pre_grads = jnp.stack([gate_grad, up_grad], axis=2)
    out_part = jnp.sum(
        jnp.einsum("eth,edh->etd", hidden, weights_down, preferred_element_type=F32), axis=0
    ).astype(BF16)
    in_part = jnp.sum(
        jnp.einsum("etgh,edgh->etd", pre_grads, weights_gate_up, preferred_element_type=F32), axis=0
    ).astype(BF16)
    both = jnp.stack([out_part, in_part]).reshape(
        2, n_expert, tok_rows, n_tensor, width // n_tensor
    )
    both = both.transpose(1, 3, 0, 2, 4).reshape(
        n_expert * n_tensor, 2, tok_rows, width // n_tensor
    )
    back = lax.all_to_all(both, ("expert", "tensor"), split_axis=0, concat_axis=0, tiled=True)
    results = jnp.sum(back.astype(F32), axis=0).astype(BF16)
    rows = jnp.concatenate(sides, axis=0)
    gate_up_grad = jnp.einsum(
        "td,geth->edgh", rows[:, :share], acts[:2], preferred_element_type=F32
    ).astype(BF16)
    down_grad = jnp.einsum(
        "td,eth->edh", rows[:, share:], acts[2], preferred_element_type=F32
    ).astype(BF16)
    return (results[0], results[1], gate_up_grad, down_grad)


def solution(mesh):
    return jax.shard_map(
        body,
        mesh=mesh,
        in_specs=(
            P(("dp", "expert"), None),
            P(("dp", "expert"), None),
            P(("dp", "expert"), None),
            P("expert", None, None, "tensor"),
            P("expert", None, "tensor"),
            P(("dp", "expert"), None),
        ),
        out_specs=(
            P(("dp", "expert"), "tensor"),
            P(("dp", "expert"), "tensor"),
            P("expert", "dp", None, "tensor"),
            P("expert", "dp", "tensor"),
        ),
        check_vma=False,
    )
```

profile of v0, /device:TPU:0, one launch (start us, length us, event | category | flops | bytes accessed | tf_op | source)
XLA Modules:
  0.0 121.2 jit_solution(4500048296995259462)
XLA Ops:
  7.2 0.0 copy-start
  7.2 0.0 all-gather.2.cloned.1.call-start
  7.2 0.9 copy.62
  8.1 0.8 copy.63
  8.9 0.1 select_reduce_fusion
  9.0 0.1 fusion.56
  9.1 1.5 %pad_maximum_fusion.4 = bf16[16,4224]{1,0:T(8,128)(2,1)} fusion(bf16[16,128]{1,0:T(8,128)(2,1)S(1)} %fusion.56, bf16[16,2048]{1,0:T(8,128)(2,1)} %param.11, bf16[16,2048]{1,0:T(8,128)(2,1)} %param.6), kind=kLoop, calls=%fused_computation.63 | loop fusion | flops 405504 | bytes 270336 | tf_op jit(solution)/shard_map/concatenate | solution.py:31
  10.6 0.0 all-gather.2.cloned.1.call-update
  10.7 25.1 %all-gather.2.cloned.1.call-done = bf16[128,4224]{1,0:T(8,128)(2,1)} async-done(((bf16[16,4224]{1,0:T(8,128)(2,1)}), bf16[128,4224]{1,0:T(8,128)(2,1)}) %all-gather.2.cloned.1.call-update) | async-done | bytes 1081360 | tf_op jit(solution)/shard_map/all_gather | solution.py:32
  35.8 0.8 slice.59
  36.6 0.1 copy.80
  36.7 4.0 %fusion.12 = f32[2,128,2,384]{3,1,2,0:T(8,128)S(1)} fusion(bf16[2,2048,2,384]{3,2,1,0:T(2,128)(2,1)} %param.9, bf16[128,4224]{1,0:T(8,128)(2,1)} %all-gather.2.cloned.1.call-done), kind=kOutput, calls=%fused_computation.11 | convolution fusion | flops 805306368 | bytes 7602176 | tf_op jit(solution)/shard_map/td,edgh->etgh/dot_general | solution.py:57
  40.7 0.0 copy-start.4
  40.7 0.9 copy-done.4
  41.5 0.0 copy-done
  41.5 2.0 %fusion.7 = bf16[128,2048]{1,0:T(8,128)(2,1)} fusion(bf16[2,2048,384]{2,1,0:T(8,128)(2,1)S(1)} %copy-done, f32[2,128,2,384]{3,1,2,0:T(8,128)S(1)} %fusion.12, f32[2,128]{1,0:T(2,128)S(1)} %fusion.58), kind=kOutput, calls=%fused_computation.7 | convolution fusion | flops 403603456 | bytes 4457472 | tf_op jit(solution)/shard_map/eth,edh->etd/dot_general | solution.py:70
  43.5 2.2 %stack.28 = bf16[1,8,16,2,1024]{4,3,2,1,0:T(2,128)(2,1)} reshape(bf16[128,2048]{1,0:T(8,128)(2,1)} %fusion.7) | data formatting | bytes 1048576 | tf_op jit(solution)/shard_map/stack | solution.py:75
  45.7 2.0 %copy.68 = bf16[1,8,16,2,1024]{4,2,0,3,1:T(8,128)(2,1)} copy(bf16[1,8,16,2,1024]{4,3,2,1,0:T(2,128)(2,1)} %stack.28) | data formatting | bytes 1048576 | tf_op jit(solution)/shard_map/stack | solution.py:75
  47.7 1.9 %fusion.44 = (bf16[2,128,384]{2,1,0:T(8,128)(2,1)S(1)}, bf16[2,128,384]{2,1,0:T(8,128)(2,1)S(1)}) fusion(f32[2,128,2,384]{3,1,2,0:T(8,128)} %copy-done.4, bf16[2,2048,384]{2,1,0:T(8,128)(2,1)S(1)} %copy-done, bf16[128,4224]{1,0:T(8,128)(2,1)} %all-gather.2.cloned.1.call-done, f32[2,128]{1,0:T(2,128)S(1)} %fusion.58), kind=kOutput, calls=%fused_computation.54 | convolution fusion | flops 404029440 | bytes 4850688 | tf_op jit(solution)/shard_map/td,edh->eth/dot_general | solution.py:63
  49.7 0.0 copy-start.2
  49.7 0.7 copy-done.2
  50.4 5.8 %fusion.8 = bf16[128,2048]{1,0:T(8,128)(2,1)} fusion(bf16[2,2048,2,384]{3,2,1,0:T(2,128)(2,1)} %param.9, bf16[2,128,1,384]{3,1,0,2:T(8,128)(2,1)S(1)} %bitcast.126, bf16[2,128,1,384]{3,1,0,2:T(8,128)(2,1)S(1)} %bitcast.122), kind=kOutput, calls=%fused_computation.8 | convolution fusion | flops 805765120 | bytes 7208960 | tf_op jit(solution)/shard_map/etgh,edgh->etd/dot_general | solution.py:73
  56.2 2.2 %stack.32 = bf16[1,8,16,2,1024]{4,3,2,1,0:T(2,128)(2,1)} reshape(bf16[128,2048]{1,0:T(8,128)(2,1)} %fusion.8) | data formatting | bytes 1048576 | tf_op jit(solution)/shard_map/stack | solution.py:75
  58.4 1.2 copy.69
  59.6 2.1 %pad_maximum_fusion = bf16[2,8,16,2,1024]{4,2,0,3,1:T(8,128)(2,1)} fusion(bf16[1,8,16,2,1024]{4,2,0,3,1:T(8,128)(2,1)S(1)} %copy.69, bf16[1,8,16,2,1024]{4,2,0,3,1:T(8,128)(2,1)} %copy.68), kind=kLoop, calls=%fused_computation.21 | loop fusion | flops 524288 | bytes 2097152 | tf_op jit(solution)/shard_map/stack | solution.py:75
  61.7 4.4 %all-to-all-start = ((bf16[16,2,16,1024]{3,2,1,0:T(8,128)(2,1)}), bf16[16,2,16,1024]{3,2,1,0:T(8,128)(2,1)}, u32[]{:S(2)}, u32[]{:S(2)}) async-start(bf16[16,2,16,1024]{3,2,1,0:T(8,128)(2,1)} %bitcast.121), calls=%async_computation | async-start | bytes 2097152 | tf_op jit(solution)/shard_map/all_to_all | solution.py:81
  66.1 0.0 copy-start.5
  66.2 1.3 %fusion.66 = (bf16[128,2048]{1,0:T(8,128)(2,1)S(1)}, bf16[128,2048]{1,0:T(8,128)(2,1)S(1)}) fusion(bf16[128,4224]{1,0:T(8,128)(2,1)} %all-gather.2.cloned.1.call-done), kind=kLoop, calls=%fused_computation.95 | loop fusion | bytes 2097152 | tf_op jit(solution)/shard_map/slice | solution.py:33
  67.5 0.0 copy-start.3
  67.5 0.1 constant_dynamic-slice_fusion.4
  67.7 1.5 %collective-permute-start.1 = (bf16[128,2048]{1,0:T(8,128)(2,1)S(1)}, bf16[128,2048]{1,0:T(8,128)(2,1)S(1)}, u32[]{:S(2)}, u32[]{:S(2)}) collective-permute-start(bf16[128,2048]{1,0:T(8,128)(2,1)S(1)} %pad_maximum_fusion.3), channel_id=1, source_target_pairs={{0,16},{16,0},{1,17},{17,1},{2,18},{18,2},{3,19},{19,3},{4,20},{20... | collective-permute-start | bytes 1572872 | tf_op jit(solution)/shard_map/ppermute | solution.py:54
  69.2 0.0 copy-done.5
  69.2 0.1 fusion.48
  69.3 0.0 copy-done.3
  69.3 0.1 pad_maximum_fusion.2
  69.4 0.6 collective-permute-start
  70.1 12.4 %collective-permute-done.1 = bf16[128,2048]{1,0:T(8,128)(2,1)S(1)} collective-permute-done((bf16[128,2048]{1,0:T(8,128)(2,1)S(1)}, bf16[128,2048]{1,0:T(8,128)(2,1)S(1)}, u32[]{:S(2)}, u32[]{:S(2)}) %collective-permute-start.1) | collective-permute-done | bytes 524320 | tf_op jit(solution)/shard_map/ppermute | solution.py:54
  82.5 0.1 pad_maximum_fusion.1
  82.6 0.0 copy-start.1
  82.6 12.0 %collective-permute-done = bf16[3,2,128,384]{3,2,1,0:T(8,128)(2,1)S(1)} collective-permute-done((bf16[3,2,128,384]{3,2,1,0:T(8,128)(2,1)S(1)}, bf16[3,2,128,384]{3,2,1,0:T(8,128)(2,1)S(1)}, u32[]{:S(2)}, u32[]{:S(2)}) %collective-permute-start) | collective-permute-done | bytes 589856 | tf_op jit(solution)/shard_map/ppermute | solution.py:54
  94.5 0.0 copy-done.1
  94.6 0.0 copy-start.6
  94.6 0.8 copy-done.6
  95.4 1.8 %fusion.11 = bf16[2,1024,384]{1,2,0:T(8,128)(2,1)} fusion(bf16[256,2048]{1,0:T(8,128)(2,1)S(1)} %pad_maximum_fusion.1, bf16[3,2,128,384]{3,2,1,0:T(8,128)(2,1)S(1)} %collective-permute-done, bf16[1,2,128,384]{3,2,1,0:T(8,128)(2,1)S(1)} %fusion.48, bf16[1,2,128,384]{3,2,1,0:T(8,128)(2,1)S(1)} %bitcast.129, bf16[1,2,128,384]{3,2,1,0:T(8,128)(2,1)S(1)} %bitcast.124), kind=kOutput, calls=%fused_computation.10 | convolution fusion | flops 405012480 | bytes 3276800 | tf_op jit(solution)/shard_map/td,eth->edh/dot_general | solution.py:87
  97.1 2.6 %copy.73 = bf16[2,1024,384]{2,1,0:T(8,128)(2,1)} copy(bf16[2,1024,384]{1,2,0:T(8,128)(2,1)} %fusion.11) | data formatting | bytes 3145728
  99.7 3.9 %convert_bitcast_fusion = bf16[2,1024,2,384]{1,3,0,2:T(8,128)(2,1)} fusion(bf16[3,2,128,384]{3,2,1,0:T(8,128)(2,1)} %copy-done.6, bf16[1,2,128,384]{3,2,1,0:T(8,128)(2,1)S(1)} %fusion.48, bf16[1,2,128,384]{3,2,1,0:T(8,128)(2,1)} %bitcast.127, bf16[1,2,128,384]{3,2,1,0:T(8,128)(2,1)S(1)} %bitcast.125, bf16[256,2048]{1,0:T(8,128)(2,1)} %copy-done.1), kind=kOutput, calls=%fused_computation.4 | convolution fusion | flops 811597824 | bytes 4849664 | tf_op jit(solution)/shard_map/td,geth->edgh/dot_general | solution.py:84
  103.6 8.7 %copy.72 = bf16[2,1024,2,384]{3,2,1,0:T(2,128)(2,1)} copy(bf16[2,1024,2,384]{1,3,0,2:T(8,128)(2,1)} %convert_bitcast_fusion) | data formatting | bytes 6291456
  112.3 0.0 all-to-all-done
  112.3 1.4 %reduce_sum.23 = bf16[2,16,1024]{2,1,0:T(8,128)(2,1)S(1)} reduce(bf16[16,2,16,1024]{3,2,1,0:T(8,128)(2,1)} %all-to-all-done, bf16[]{:T(256)} %constant.23.clone.1), dimensions={0}, to_apply=%region_1.2 | reduce | flops 491520 | bytes 1114114 | tf_op jit(solution)/shard_map/reduce_sum | solution.py:82
  113.7 0.6 slice_bitcast_fusion.4
  (4 shorter events, 0.1 us)
Async XLA Ops:
  7.2 34.4 %copy-start = (bf16[2,2048,384]{2,1,0:T(8,128)(2,1)S(1)}, bf16[2,2048,384]{2,1,0:T(8,128)(2,1)}, u32[]{:S(2)}) copy-start(bf16[2,2048,384]{2,1,0:T(8,128)(2,1)} %param.10) | copy-start | bytes 9437188
  7.2 28.6 %all-gather.2.cloned.1.call-start = ((), (), s32[]{:S(2)}) async-start(), calls=%async_computation.1 | async-start | bytes 1216512 | tf_op jit(solution)/shard_map/all_gather | solution.py:32
  40.7 0.9 copy-start.4
  49.7 0.7 copy-start.2
  61.7 50.6 %all-to-all-start = ((bf16[16,2,16,1024]{3,2,1,0:T(8,128)(2,1)}), bf16[16,2,16,1024]{3,2,1,0:T(8,128)(2,1)}, u32[]{:S(2)}, u32[]{:S(2)}) async-start(bf16[16,2,16,1024]{3,2,1,0:T(8,128)(2,1)} %bitcast.121), calls=%async_computation | async-start | bytes 2097152 | tf_op jit(solution)/shard_map/all_to_all | solution.py:81
  66.1 3.0 %copy-start.5 = (f32[2,128,2,384]{3,1,2,0:T(8,128)S(1)}, f32[2,128,2,384]{3,1,2,0:T(8,128)}, u32[]{:S(2)}) copy-start(f32[2,128,2,384]{3,1,2,0:T(8,128)} %copy-done.4) | copy-start | bytes 2359300
  67.5 1.8 %copy-start.3 = (bf16[2,128,384]{2,1,0:T(8,128)(2,1)S(1)}, bf16[2,128,384]{2,1,0:T(8,128)(2,1)}, u32[]{:S(2)}) copy-start(bf16[2,128,384]{2,1,0:T(8,128)(2,1)} %copy-done.2) | copy-start | bytes 589828
  67.7 14.8 %collective-permute-start.1 = (bf16[128,2048]{1,0:T(8,128)(2,1)S(1)}, bf16[128,2048]{1,0:T(8,128)(2,1)S(1)}, u32[]{:S(2)}, u32[]{:S(2)}) collective-permute-start(bf16[128,2048]{1,0:T(8,128)(2,1)S(1)} %pad_maximum_fusion.3), channel_id=1, source_target_pairs={{0,16},{16,0},{1,17},{17,1},{2,18},{18,2},{3,19},{19,3},{4,20},{20... | collective-permute-start | bytes 1572872 | tf_op jit(solution)/shard_map/ppermute | solution.py:54
  69.4 25.1 %collective-permute-start = (bf16[3,2,128,384]{3,2,1,0:T(8,128)(2,1)S(1)}, bf16[3,2,128,384]{3,2,1,0:T(8,128)(2,1)S(1)}, u32[]{:S(2)}, u32[]{:S(2)}) collective-permute-start(bf16[3,2,128,384]{3,2,1,0:T(8,128)(2,1)S(1)} %pad_maximum_fusion.2), channel_id=1, source_target_pairs={{0,16},{16,0},{1,17},{17,1},{2,18},{18,2},{3,19},{19,3},{4,20},{20... | collective-permute-start | bytes 1769480 | tf_op jit(solution)/shard_map/ppermute | solution.py:54
  82.6 12.0 %copy-start.1 = (bf16[256,2048]{1,0:T(8,128)(2,1)}, bf16[256,2048]{1,0:T(8,128)(2,1)S(1)}, u32[]{:S(2)}) copy-start(bf16[256,2048]{1,0:T(8,128)(2,1)S(1)} %pad_maximum_fusion.1) | copy-start | bytes 3145732
  94.6 0.8 copy-start.6
Sparse Core Ops, SparseCore 0:
  10.8 24.9 all-gather.1
where the time goes:
time: 122 us; the launch traced here: 121 us
  waiting for transfers between devices  49.5 us (41%)
  local copies, waits for them, and re-layouts  25.9 us (21%)
  matrix products  19.3 us (16%)
  between operations  14.2 us (12%)
  starting transfers between devices  6.63 us (5%)
  other arithmetic  5.65 us (5%)
    all_gather x1, waiting for transfers between devices, body(): held = lax.all_gather(sent, 'expert', axis=0, tiled=True)  25.1 us
    ppermute x2, waiting for transfers between devices, moved(): lax.ppermute(value, 'dp', [(i, (i + shift) % n_dp) for i in range(n_dp)])  24.4 us
    unnamed x19, local copies, waits for them, and re-layouts  15.4 us
    another operation x4, local copies, waits for them, and re-layouts, body(): jnp.stack([out_part, in_part])  7.64 us
    dot_general x1, matrix products, body(): jnp.einsum('etgh,edgh->etd', pre_grads, weights_gate_up, preferred_elemen...  5.78 us
    all_to_all x1, starting transfers between devices, body(): lax.all_to_all(both, ('expert', 'tensor'), split_axis=0, concat_axis=0, t...  4.42 us
    dot_general x1, matrix products, body(): jnp.einsum('td,edgh->etgh', tok, weights_gate_up, preferred_element_type=...  3.95 us
    dot_general x1, matrix products, body(): jnp.einsum('td,geth->edgh', rows[:, :share], acts[:2], preferred_element_...  3.9 us
  transfers between devices with their start and end apart: 4, of which 3 were waited for; matrix products, arithmetic and copies ran while one was open for 15% of the time, Pallas kernels for 0%

commit v1 on v0

--- a/solution.py
+++ b/solution.py
@@ -1,3 +1,4 @@
+import functools
 import jax
 import jax.numpy as jnp
 from jax import lax
@@ -5,6 +6,38 @@
 
 F32 = jnp.float32
 BF16 = jnp.bfloat16
+
+
+def ends_shape(local_values, axis_tag, axis_k):
+    carry, r_now, left_arr = (
+        lax.axis_size(axis_tag),
+        lax.axis_index(axis_tag),
+        local_values.shape[axis_k],
+    )
+    tmp = lax.dynamic_update_slice_in_dim(
+        jnp.zeros(
+            [j0 * carry if k == axis_k else j0 for k, j0 in enumerate(local_values.shape)],
+            local_values.dtype,
+        ),
+        local_values,
+        r_now * left_arr,
+        axis=axis_k,
+    )
+    high = x_new = local_values
+    for c in range(1, carry // 2 + 1):
+        high = lax.ppermute(high, axis_tag, [(k, (k + 1) % carry) for k in range(carry)])
+        tmp = lax.dynamic_update_slice_in_dim(
+            tmp, high, (r_now - c) % carry * left_arr, axis=axis_k
+        )
+        if 2 * c < carry:
+            x_new = lax.ppermute(x_new, axis_tag, [(k, (k - 1) % carry) for k in range(carry)])
+            tmp = lax.dynamic_update_slice_in_dim(
+                tmp, x_new, (r_now + c) % carry * left_arr, axis=axis_k
+            )
+    return tmp
+
+
+_pass_tails = functools.partial(ends_shape, axis_tag="expert", axis_k=0)
 
 
 def cut(value):
@@ -29,7 +62,7 @@
     spare = -parts.shape[1] % 128
     parts = jnp.pad(parts, ((0, 0), (0, spare)))
     sent = jnp.concatenate([tokens, cotangent, parts], axis=1)
-    held = lax.all_gather(sent, "expert", axis=0, tiled=True)
+    held = _pass_tails(sent)
     tok = held[:, :width]
     cot = held[:, width : 2 * width]
     parts = held[:, 2 * width : 2 * width + 3 * expert_total].astype(F32)

time: 122 us -> 220 us (1.80); the launches traced: 121 us -> 216 us
  local copies, waits for them, and re-layouts: 25.9 us -> 139 us
  waiting for transfers between devices: 49.5 us -> 33 us
  starting transfers between devices: 6.63 us -> 21.1 us
  between operations: 14.2 us -> 0.86 us
  matrix products: 19.3 us -> 16.7 us
    dynamic_update_slice x0 -> x8, local copies, waits for them, and re-layouts: none -> 100 us  [the longest x4 51 us: ends_shape(): lax.dynamic_update_slice_in_dim(tmp, high, (r_now - c) % carry * left_arr...]
    all_gather x1 -> x0, waiting for transfers between devices: 25.1 us -> none  [body(): held = lax.all_gather(sent, 'expert', axis=0, tiled=True)]
    ppermute x0 -> x7, local copies, waits for them, and re-layouts: none -> 12.3 us  [the longest x4 7.29 us: ends_shape(): lax.ppermute(high, axis_tag, [(k, (k + 1) % carry) for k in range(carry)])]
    ppermute x0 -> x7, starting transfers between devices: none -> 11.9 us  [the longest x3 11.3 us: ends_shape(): lax.ppermute(x_new, axis_tag, [(k, (k - 1) % carry) for k in range(carry)])]
    ppermute x0 -> x7, waiting for transfers between devices: none -> 9.04 us  [the longest x4 8.96 us: ends_shape(): lax.ppermute(high, axis_tag, [(k, (k + 1) % carry) for k in range(carry)])]
    dot_general x1, matrix products: 5.78 us -> 3.02 us  [body(): jnp.einsum('etgh,edgh->etd', pre_grads, weights_gate_up, preferred_elemen...]
    all_to_all x1, starting transfers between devices: 4.42 us -> 6.74 us  [body(): lax.all_to_all(both, ('expert', 'tensor'), split_axis=0, concat_axis=0, t...]
    unnamed x19 -> x32, local copies, waits for them, and re-layouts: 15.4 us -> 13.9 us
  transfers between devices with their start and end apart: 4 -> 10, of which waited for: 3 -> 6; matrix products, arithmetic and copies ran while one was open for 15% -> 55% of each run, Pallas kernels for 0% -> 0%
where the time goes in v1:
time: 220 us; the launch traced here: 216 us
  local copies, waits for them, and re-layouts  139 us (63%)
  waiting for transfers between devices  33 us (15%)
  starting transfers between devices  21.1 us (10%)
  matrix products  16.7 us (8%)
  other arithmetic  4.99 us (2%)
    dynamic_update_slice x4, local copies, waits for them, and re-layouts, ends_shape(): lax.dynamic_update_slice_in_dim(tmp, high, (r_now - c) % carry * left_arr...  51 us
    dynamic_update_slice x3, local copies, waits for them, and re-layouts, ends_shape(): lax.dynamic_update_slice_in_dim(tmp, x_new, (r_now + c) % carry * left_ar...  38.3 us
    ppermute x2, waiting for transfers between devices, moved(): lax.ppermute(value, 'dp', [(i, (i + shift) % n_dp) for i in range(n_dp)])  24 us
    unnamed x32, local copies, waits for them, and re-layouts  13.9 us
    ppermute x3, starting transfers between devices, ends_shape(): lax.ppermute(x_new, axis_tag, [(k, (k - 1) % carry) for k in range(carry)])  11.3 us
    dynamic_update_slice x1, local copies, waits for them, and re-layouts, ends_shape(): lax.dynamic_update_slice_in_dim(jnp.zeros([j0 * carry if k == axis_k else...  10.9 us
    ppermute x4, waiting for transfers between devices, ends_shape(): lax.ppermute(high, axis_tag, [(k, (k + 1) % carry) for k in range(carry)])  8.96 us
    another operation x4, local copies, waits for them, and re-layouts, body(): jnp.stack([out_part, in_part])  7.58 us
  transfers between devices with their start and end apart: 10, of which 6 were waited for; matrix products, arithmetic and copies ran while one was open for 55% of the time, Pallas kernels for 0%

profile of v1, /device:TPU:0, one launch (start us, length us, event | category | flops | bytes accessed | tf_op | source)
XLA Modules:
  0.0 215.7 jit_solution(3481987651661811042)
XLA Ops:
  0.6 0.0 copy-start
  0.6 0.9 copy.63
  1.6 0.8 copy.62
  2.4 0.1 select_reduce_fusion
  2.5 0.1 fusion.56
  2.6 0.9 pad_maximum_fusion.4
  3.5 0.5 collective-permute-start
  4.0 4.1 %collective-permute-start.1 = (bf16[16,4224]{1,0:T(8,128)(2,1)S(1)}, bf16[16,4224]{1,0:T(8,128)(2,1)S(1)}, u32[]{:S(2)}, u32[]{:S(2)}) collective-permute-start(bf16[16,4224]{1,0:T(8,128)(2,1)S(1)} %pad_maximum_fusion.4), channel_id=1, source_target_pairs={{0,14},{2,0},{4,2},{6,4},{8,6},{10,8},{12,10},{14,12},{1,15},{3,1}... | collective-permute-start | bytes 405512 | tf_op jit(solution)/shard_map/ppermute | solution.py:33
  8.1 2.7 %collective-permute-done = bf16[16,4224]{1,0:T(8,128)(2,1)S(1)} collective-permute-done((bf16[16,4224]{1,0:T(8,128)(2,1)S(1)}, bf16[16,4224]{1,0:T(8,128)(2,1)S(1)}, u32[]{:S(2)}, u32[]{:S(2)}) %collective-permute-start) | collective-permute-done | bytes 135200 | tf_op jit(solution)/shard_map/ppermute | solution.py:28
  10.8 0.0 collective-permute-start.2
  10.8 0.0 collective-permute-done.1
  10.8 3.5 %collective-permute-start.3 = (bf16[16,4224]{1,0:T(8,128)(2,1)S(1)}, bf16[16,4224]{1,0:T(8,128)(2,1)S(1)}, u32[]{:S(2)}, u32[]{:S(2)}) collective-permute-start(bf16[16,4224]{1,0:T(8,128)(2,1)S(1)} %collective-permute-done.1), channel_id=1, source_target_pairs={{0,14},{2,0},{4,2},{6,4},{8,6},{10,8},{12,10},{14,12},{1,15},{3,1}... | collective-permute-start | bytes 405512 | tf_op jit(solution)/shard_map/ppermute | solution.py:33
  14.3 3.5 %collective-permute-done.2 = bf16[16,4224]{1,0:T(8,128)(2,1)S(1)} collective-permute-done((bf16[16,4224]{1,0:T(8,128)(2,1)S(1)}, bf16[16,4224]{1,0:T(8,128)(2,1)S(1)}, u32[]{:S(2)}, u32[]{:S(2)}) %collective-permute-start.2) | collective-permute-done | bytes 135200 | tf_op jit(solution)/shard_map/ppermute | solution.py:28
  17.8 0.1 collective-permute-done.3
  17.9 3.7 %collective-permute-start.5 = (bf16[16,4224]{1,0:T(8,128)(2,1)S(1)}, bf16[16,4224]{1,0:T(8,128)(2,1)}, u32[]{:S(2)}, u32[]{:S(2)}) collective-permute-start(bf16[16,4224]{1,0:T(8,128)(2,1)S(1)} %collective-permute-done.3), channel_id=1, source_target_pairs={{0,14},{2,0},{4,2},{6,4},{8,6},{10,8},{12,10},{14,12},{1,15},{3,1}... | collective-permute-start | bytes 405512 | tf_op jit(solution)/shard_map/ppermute | solution.py:33
  21.6 2.8 %collective-permute-done.4 = bf16[16,4224]{1,0:T(8,128)(2,1)S(1)} collective-permute-done((bf16[16,4224]{1,0:T(8,128)(2,1)S(1)}, bf16[16,4224]{1,0:T(8,128)(2,1)S(1)}, u32[]{:S(2)}, u32[]{:S(2)}) %collective-permute-start.4) | collective-permute-done | bytes 135200 | tf_op jit(solution)/shard_map/ppermute | solution.py:28
  24.4 1.4 copy.64
  25.7 1.1 broadcast_in_dim.19
  26.9 10.9 %dynamic_update_slice.24 = bf16[128,4224]{0,1:T(8,128)(2,1)} dynamic-update-slice(bf16[128,4224]{0,1:T(8,128)(2,1)} %broadcast_in_dim.19, bf16[16,4224]{0,1:T(8,128)(2,1)} %copy.64, s32[]{:T(128)S(6)} %select_n.71, s32[]{:T(128)} %constant.69.clone.1) | dynamic-update-slice | bytes 270340 | tf_op jit(solution)/shard_map/dynamic_update_slice | solution.py:17
  37.7 2.3 %copy.65 = bf16[16,4224]{0,1:T(8,128)(2,1)} copy(bf16[16,4224]{1,0:T(8,128)(2,1)} %copy-done.11) | data formatting | bytes 270336 | tf_op jit(solution)/shard_map/ppermute | solution.py:28
  40.0 12.7 %dynamic_update_slice.25 = bf16[128,4224]{0,1:T(8,128)(2,1)} dynamic-update-slice(bf16[128,4224]{0,1:T(8,128)(2,1)} %dynamic_update_slice.24, bf16[16,4224]{0,1:T(8,128)(2,1)} %copy.65, s32[]{:T(128)S(6)} %select_n.73, s32[]{:T(128)} %constant.69.clone.1) | dynamic-update-slice | bytes 270340 | tf_op jit(solution)/shard_map/dynamic_update_slice | solution.py:29
  52.8 1.4 copy.66
  54.1 12.8 %dynamic_update_slice.26 = bf16[128,4224]{0,1:T(8,128)(2,1)} dynamic-update-slice(bf16[128,4224]{0,1:T(8,128)(2,1)} %dynamic_update_slice.25, bf16[16,4224]{0,1:T(8,128)(2,1)} %copy.66, s32[]{:T(128)S(6)} %select_n.75, s32[]{:T(128)} %constant.69.clone.1) | dynamic-update-slice | bytes 270340 | tf_op jit(solution)/shard_map/dynamic_update_slice | solution.py:34
  66.9 1.4 copy.67
  68.3 12.7 %dynamic_update_slice.27 = bf16[128,4224]{0,1:T(8,128)(2,1)} dynamic-update-slice(bf16[128,4224]{0,1:T(8,128)(2,1)} %dynamic_update_slice.26, bf16[16,4224]{0,1:T(8,128)(2,1)} %copy.67, s32[]{:T(128)S(6)} %select_n.77, s32[]{:T(128)} %constant.69.clone.1) | dynamic-update-slice | bytes 270340 | tf_op jit(solution)/shard_map/dynamic_update_slice | solution.py:29
  81.0 1.4 copy.68
  82.4 12.7 %dynamic_update_slice.28 = bf16[128,4224]{0,1:T(8,128)(2,1)} dynamic-update-slice(bf16[128,4224]{0,1:T(8,128)(2,1)} %dynamic_update_slice.27, bf16[16,4224]{0,1:T(8,128)(2,1)} %copy.68, s32[]{:T(128)S(6)} %select_n.79, s32[]{:T(128)} %constant.69.clone.1) | dynamic-update-slice | bytes 270340 | tf_op jit(solution)/shard_map/dynamic_update_slice | solution.py:34
  95.1 1.4 copy.69
  96.5 12.7 %dynamic_update_slice.29 = bf16[128,4224]{0,1:T(8,128)(2,1)} dynamic-update-slice(bf16[128,4224]{0,1:T(8,128)(2,1)} %dynamic_update_slice.28, bf16[16,4224]{0,1:T(8,128)(2,1)} %copy.69, s32[]{:T(128)S(6)} %select_n.81, s32[]{:T(128)} %constant.69.clone.1) | dynamic-update-slice | bytes 270340 | tf_op jit(solution)/shard_map/dynamic_update_slice | solution.py:29
  109.2 2.3 %copy.70 = bf16[16,4224]{0,1:T(8,128)(2,1)} copy(bf16[16,4224]{1,0:T(8,128)(2,1)} %collective-permute-done.5) | data formatting | bytes 270336 | tf_op jit(solution)/shard_map/ppermute | solution.py:33
  111.5 12.7 %dynamic_update_slice.30 = bf16[128,4224]{0,1:T(8,128)(2,1)} dynamic-update-slice(bf16[128,4224]{0,1:T(8,128)(2,1)} %dynamic_update_slice.29, bf16[16,4224]{0,1:T(8,128)(2,1)} %copy.70, s32[]{:T(128)S(6)} %select_n.83, s32[]{:T(128)} %constant.69.clone.1) | dynamic-update-slice | bytes 270340 | tf_op jit(solution)/shard_map/dynamic_update_slice | solution.py:34
  124.2 2.3 %copy.71 = bf16[16,4224]{0,1:T(8,128)(2,1)} copy(bf16[16,4224]{1,0:T(8,128)(2,1)} %collective-permute-done.6) | data formatting | bytes 270336 | tf_op jit(solution)/shard_map/ppermute | solution.py:28
  126.5 12.7 %dynamic_update_slice.31 = bf16[128,4224]{0,1:T(8,128)(2,1)} dynamic-update-slice(bf16[128,4224]{0,1:T(8,128)(2,1)} %dynamic_update_slice.30, bf16[16,4224]{0,1:T(8,128)(2,1)} %copy.71, s32[]{:T(128)S(6)} %select_n.85, s32[]{:T(128)} %constant.69.clone.1) | dynamic-update-slice | bytes 270340 | tf_op jit(solution)/shard_map/dynamic_update_slice | solution.py:29
  139.2 0.7 slice.59
  139.9 4.1 %fusion.12 = f32[2,128,2,384]{3,1,2,0:T(8,128)S(1)} fusion(bf16[2,2048,2,384]{3,2,1,0:T(2,128)(2,1)} %param.9, bf16[128,4224]{0,1:T(8,128)(2,1)} %dynamic_update_slice.31), kind=kOutput, calls=%fused_computation.11 | convolution fusion | flops 805306368 | bytes 7602176 | tf_op jit(solution)/shard_map/td,edgh->etgh/dot_general | solution.py:90
  144.0 0.0 copy-start.4
  144.1 0.0 slice-start.1
  144.1 2.0 fusion.44
  146.2 2.0 fusion.7
  148.1 3.0 %fusion.8 = bf16[128,2048]{1,0:T(8,128)(2,1)} fusion(bf16[2,2048,2,384]{3,2,1,0:T(2,128)(2,1)S(1)} %bitcast.128, bf16[2,128,1,384]{3,1,0,2:T(8,128)(2,1)S(1)} %bitcast.122, bf16[2,128,1,384]{3,1,0,2:T(8,128)(2,1)S(1)} %bitcast.118), kind=kOutput, calls=%fused_computation.8 | convolution fusion | flops 805765120 | bytes 7208960 | tf_op jit(solution)/shard_map/etgh,edgh->etd/dot_general | solution.py:106
  151.2 2.2 %stack.32 = bf16[1,8,16,2,1024]{4,3,2,1,0:T(2,128)(2,1)} reshape(bf16[128,2048]{1,0:T(8,128)(2,1)} %fusion.8) | data formatting | bytes 1048576 | tf_op jit(solution)/shard_map/stack | solution.py:108
  153.4 2.0 copy.78
  155.4 2.2 %stack.28 = bf16[1,8,16,2,1024]{4,3,2,1,0:T(2,128)(2,1)} reshape(bf16[128,2048]{1,0:T(8,128)(2,1)} %fusion.7) | data formatting | bytes 1048576 | tf_op jit(solution)/shard_map/stack | solution.py:108
  157.6 1.2 copy.77
  158.7 2.1 pad_maximum_fusion
  160.9 6.7 %all-to-all-start = ((bf16[16,2,16,1024]{3,2,1,0:T(8,128)(2,1)}), bf16[16,2,16,1024]{3,2,1,0:T(8,128)(2,1)}, u32[]{:S(2)}, u32[]{:S(2)}) async-start(bf16[16,2,16,1024]{3,2,1,0:T(8,128)(2,1)} %bitcast.117), calls=%async_computation | async-start | bytes 2097152 | tf_op jit(solution)/shard_map/all_to_all | solution.py:114
  167.6 1.3 fusion.66
  168.9 0.0 copy-start.5
  168.9 0.1 constant_dynamic-slice_fusion.4
  169.0 1.6 collective-permute-start.8
  170.6 0.1 fusion.48
  170.7 0.1 pad_maximum_fusion.2
  170.8 1.0 collective-permute-start.7
  171.8 12.0 %collective-permute-done.8 = bf16[128,2048]{0,1:T(8,128)(2,1)S(1)} collective-permute-done((bf16[128,2048]{0,1:T(8,128)(2,1)S(1)}, bf16[128,2048]{0,1:T(8,128)(2,1)S(1)}, u32[]{:S(2)}, u32[]{:S(2)}) %collective-permute-start.8) | collective-permute-done | bytes 524320 | tf_op jit(solution)/shard_map/ppermute | solution.py:87
  183.8 0.1 pad_maximum_fusion.1
  184.0 0.0 copy-start.1
  184.0 11.9 %collective-permute-done.7 = bf16[3,2,128,384]{3,2,1,0:T(8,128)(2,1)S(1)} collective-permute-done((bf16[3,2,128,384]{3,2,1,0:T(8,128)(2,1)S(1)}, bf16[3,2,128,384]{3,2,1,0:T(8,128)(2,1)S(1)}, u32[]{:S(2)}, u32[]{:S(2)}) %collective-permute-start.7) | collective-permute-done | bytes 589856 | tf_op jit(solution)/shard_map/ppermute | solution.py:87
  195.9 0.8 copy-done.6
  196.8 2.7 %convert_bitcast_fusion = bf16[2,1024,2,384]{1,3,0,2:T(8,128)(2,1)} fusion(bf16[3,2,128,384]{3,2,1,0:T(8,128)(2,1)S(1)} %collective-permute-done.7, bf16[1,2,128,384]{3,2,1,0:T(8,128)(2,1)S(1)} %fusion.48, bf16[1,2,128,384]{3,2,1,0:T(8,128)(2,1)S(1)} %bitcast.125, bf16[1,2,128,384]{3,2,1,0:T(8,128)(2,1)S(1)} %bitcast.120, ...), kind=kOutput, calls=%fused_computation.4 | convolution fusion | flops 811597824 | bytes 4849664 | tf_op jit(solution)/shard_map/td,geth->edgh/dot_general | solution.py:117
  199.4 8.7 %copy.83 = bf16[2,1024,2,384]{3,2,1,0:T(2,128)(2,1)} copy(bf16[2,1024,2,384]{1,3,0,2:T(8,128)(2,1)} %convert_bitcast_fusion) | data formatting | bytes 6291456
  208.1 3.0 %fusion.11 = bf16[2,1024,384]{1,2,0:T(8,128)(2,1)} fusion(bf16[256,2048]{0,1:T(8,128)(2,1)} %copy-done.1, bf16[3,2,128,384]{3,2,1,0:T(8,128)(2,1)} %copy-done.6, bf16[1,2,128,384]{3,2,1,0:T(8,128)(2,1)S(1)} %fusion.48, bf16[1,2,128,384]{3,2,1,0:T(8,128)(2,1)} %bitcast.123, bf16[1,2,128,384]{3,2,1,0:T(8,128)(2,1)S(1)} %bitcast.121), kind=kOutput, calls=%fused_computation.10 | convolution fusion | flops 405012480 | bytes 3276800 | tf_op jit(solution)/shard_map/td,eth->edh/dot_general | solution.py:120
  211.1 2.6 %copy.84 = bf16[2,1024,384]{2,1,0:T(8,128)(2,1)} copy(bf16[2,1024,384]{1,2,0:T(8,128)(2,1)} %fusion.11) | data formatting | bytes 3145728
  213.6 1.4 reduce_sum.23
  215.1 0.6 slice_bitcast_fusion.4
  (32 shorter events, 0.1 us)
Async XLA Ops:
  0.6 143.5 %copy-start = (bf16[2,2048,384]{2,1,0:T(8,128)(2,1)S(1)}, bf16[2,2048,384]{2,1,0:T(8,128)(2,1)}, u32[]{:S(2)}) copy-start(bf16[2,2048,384]{2,1,0:T(8,128)(2,1)} %param.10) | copy-start | bytes 9437188
  3.5 7.3 %collective-permute-start = (bf16[16,4224]{1,0:T(8,128)(2,1)S(1)}, bf16[16,4224]{1,0:T(8,128)(2,1)S(1)}, u32[]{:S(2)}, u32[]{:S(2)}) collective-permute-start(bf16[16,4224]{1,0:T(8,128)(2,1)S(1)} %pad_maximum_fusion.4), channel_id=1, source_target_pairs={{0,2},{2,4},{4,6},{6,8},{8,10},{10,12},{12,14},{14,0},{1,3},{3,5},... | collective-permute-start | bytes 405512 | tf_op jit(solution)/shard_map/ppermute | solution.py:28
  4.0 6.8 %collective-permute-start.1 = (bf16[16,4224]{1,0:T(8,128)(2,1)S(1)}, bf16[16,4224]{1,0:T(8,128)(2,1)S(1)}, u32[]{:S(2)}, u32[]{:S(2)}) collective-permute-start(bf16[16,4224]{1,0:T(8,128)(2,1)S(1)} %pad_maximum_fusion.4), channel_id=1, source_target_pairs={{0,14},{2,0},{4,2},{6,4},{8,6},{10,8},{12,10},{14,12},{1,15},{3,1}... | collective-permute-start | bytes 405512 | tf_op jit(solution)/shard_map/ppermute | solution.py:33
  10.8 3.6 %copy-start.11 = (bf16[16,4224]{1,0:T(8,128)(2,1)}, bf16[16,4224]{1,0:T(8,128)(2,1)S(1)}, u32[]{:S(2)}) copy-start(bf16[16,4224]{1,0:T(8,128)(2,1)S(1)} %collective-permute-done) | copy-start | bytes 405508
  10.8 7.0 %collective-permute-start.2 = (bf16[16,4224]{1,0:T(8,128)(2,1)S(1)}, bf16[16,4224]{1,0:T(8,128)(2,1)S(1)}, u32[]{:S(2)}, u32[]{:S(2)}) collective-permute-start(bf16[16,4224]{1,0:T(8,128)(2,1)S(1)} %collective-permute-done), channel_id=1, source_target_pairs={{0,2},{2,4},{4,6},{6,8},{8,10},{10,12},{12,14},{14,0},{1,3},{3,5},... | collective-permute-start | bytes 405512 | tf_op jit(solution)/shard_map/ppermute | solution.py:28
  10.8 13.6 %copy-start.7 = (bf16[16,4224]{1,0:T(8,128)(2,1)}, bf16[16,4224]{1,0:T(8,128)(2,1)S(1)}, u32[]{:S(2)}) copy-start(bf16[16,4224]{1,0:T(8,128)(2,1)S(1)} %collective-permute-done.1) | copy-start | bytes 405508
  10.8 7.1 %collective-permute-start.3 = (bf16[16,4224]{1,0:T(8,128)(2,1)S(1)}, bf16[16,4224]{1,0:T(8,128)(2,1)S(1)}, u32[]{:S(2)}, u32[]{:S(2)}) collective-permute-start(bf16[16,4224]{1,0:T(8,128)(2,1)S(1)} %collective-permute-done.1), channel_id=1, source_target_pairs={{0,14},{2,0},{4,2},{6,4},{8,6},{10,8},{12,10},{14,12},{1,15},{3,1}... | collective-permute-start | bytes 405512 | tf_op jit(solution)/shard_map/ppermute | solution.py:33
  17.8 6.6 %copy-start.9 = (bf16[16,4224]{1,0:T(8,128)(2,1)}, bf16[16,4224]{1,0:T(8,128)(2,1)S(1)}, u32[]{:S(2)}) copy-start(bf16[16,4224]{1,0:T(8,128)(2,1)S(1)} %collective-permute-done.2) | copy-start | bytes 405508
  17.8 6.5 %collective-permute-start.4 = (bf16[16,4224]{1,0:T(8,128)(2,1)S(1)}, bf16[16,4224]{1,0:T(8,128)(2,1)S(1)}, u32[]{:S(2)}, u32[]{:S(2)}) collective-permute-start(bf16[16,4224]{1,0:T(8,128)(2,1)S(1)} %collective-permute-done.2), channel_id=1, source_target_pairs={{0,2},{2,4},{4,6},{6,8},{8,10},{10,12},{12,14},{14,0},{1,3},{3,5},... | collective-permute-start | bytes 405512 | tf_op jit(solution)/shard_map/ppermute | solution.py:28
  17.9 91.3 %collective-permute-start.5 = (bf16[16,4224]{1,0:T(8,128)(2,1)S(1)}, bf16[16,4224]{1,0:T(8,128)(2,1)}, u32[]{:S(2)}, u32[]{:S(2)}) collective-permute-start(bf16[16,4224]{1,0:T(8,128)(2,1)S(1)} %collective-permute-done.3), channel_id=1, source_target_pairs={{0,14},{2,0},{4,2},{6,4},{8,6},{10,8},{12,10},{14,12},{1,15},{3,1}... | collective-permute-start | bytes 405512 | tf_op jit(solution)/shard_map/ppermute | solution.py:33
  24.4 99.9 %collective-permute-start.6 = (bf16[16,4224]{1,0:T(8,128)(2,1)S(1)}, bf16[16,4224]{1,0:T(8,128)(2,1)}, u32[]{:S(2)}, u32[]{:S(2)}) collective-permute-start(bf16[16,4224]{1,0:T(8,128)(2,1)S(1)} %collective-permute-done.4), channel_id=1, source_target_pairs={{0,2},{2,4},{4,6},{6,8},{8,10},{10,12},{12,14},{14,0},{1,3},{3,5},... | collective-permute-start | bytes 405512 | tf_op jit(solution)/shard_map/ppermute | solution.py:28
  37.7 15.0 %copy-start.8 = (bf16[16,4224]{1,0:T(8,128)(2,1)S(1)}, bf16[16,4224]{1,0:T(8,128)(2,1)}, u32[]{:S(2)}) copy-start(bf16[16,4224]{1,0:T(8,128)(2,1)} %copy-done.7) | copy-start | bytes 405508
  54.1 12.8 %copy-start.10 = (bf16[16,4224]{1,0:T(8,128)(2,1)S(1)}, bf16[16,4224]{1,0:T(8,128)(2,1)}, u32[]{:S(2)}) copy-start(bf16[16,4224]{1,0:T(8,128)(2,1)} %copy-done.9) | copy-start | bytes 405508
  139.9 8.2 %slice-start = ((s8[6291456]{0:T(1024)(128)(4,1)}), s8[4194304]{0:T(1024)(128)(4,1)S(1)}, s32[]{:S(2)}) async-start(s8[6291456]{0:T(1024)(128)(4,1)} %bitcast.127), calls=%async_computation.1 | async-start | bytes 8388608
  144.0 2.1 copy-start.4
  144.1 4.0 %slice-start.1 = ((s8[6291456]{0:T(1024)(128)(4,1)}), s8[2097152]{0:T(1024)(128)(4,1)S(1)}, s32[]{:S(2)}) async-start(s8[6291456]{0:T(1024)(128)(4,1)} %bitcast.127), calls=%async_computation.2 | async-start | bytes 4194304
  146.2 2.0 copy-start.2
  160.9 52.8 %all-to-all-start = ((bf16[16,2,16,1024]{3,2,1,0:T(8,128)(2,1)}), bf16[16,2,16,1024]{3,2,1,0:T(8,128)(2,1)}, u32[]{:S(2)}, u32[]{:S(2)}) async-start(bf16[16,2,16,1024]{3,2,1,0:T(8,128)(2,1)} %bitcast.117), calls=%async_computation | async-start | bytes 2097152 | tf_op jit(solution)/shard_map/all_to_all | solution.py:114
  168.9 1.7 copy-start.5
  168.9 1.8 copy-start.3
  169.0 14.8 %collective-permute-start.8 = (bf16[128,2048]{0,1:T(8,128)(2,1)S(1)}, bf16[128,2048]{0,1:T(8,128)(2,1)S(1)}, u32[]{:S(2)}, u32[]{:S(2)}) collective-permute-start(bf16[128,2048]{0,1:T(8,128)(2,1)S(1)} %pad_maximum_fusion.3), channel_id=1, source_target_pairs={{0,16},{16,0},{1,17},{17,1},{2,18},{18,2},{3,19},{19,3},{4,20},{20... | collective-permute-start | bytes 1572872 | tf_op jit(solution)/shard_map/ppermute | solution.py:87
  170.8 25.1 %collective-permute-start.7 = (bf16[3,2,128,384]{3,2,1,0:T(8,128)(2,1)S(1)}, bf16[3,2,128,384]{3,2,1,0:T(8,128)(2,1)S(1)}, u32[]{:S(2)}, u32[]{:S(2)}) collective-permute-start(bf16[3,2,128,384]{3,2,1,0:T(8,128)(2,1)S(1)} %pad_maximum_fusion.2), channel_id=1, source_target_pairs={{0,16},{16,0},{1,17},{17,1},{2,18},{18,2},{3,19},{19,3},{4,20},{20... | collective-permute-start | bytes 1769480 | tf_op jit(solution)/shard_map/ppermute | solution.py:87
  184.0 12.0 %copy-start.1 = (bf16[256,2048]{0,1:T(8,128)(2,1)}, bf16[256,2048]{0,1:T(8,128)(2,1)S(1)}, u32[]{:S(2)}) copy-start(bf16[256,2048]{0,1:T(8,128)(2,1)S(1)} %pad_maximum_fusion.1) | copy-start | bytes 3145732
  195.9 0.8 copy-start.6
